TPU v7x, 32 devices: a whole 2x2x4 slice. The times are simulated.
32 devices in a mesh: rep: 8 (over y, x, core), shard: 4 (over z).
Axes of the slice: x: 2, y: 2, z: 4, core: 2. Of those that a mesh axis runs over, the one named last changes fastest.
Arguments:
- gradients: bfloat16 [8, 96, 2560], P(None, 'shard')
- momentum: float32 [8, 96, 2560], P(None, 'shard'), may hold values from -60 to 60
Outputs:
- updates: bfloat16 [8, 96, 2560], P(None, 'shard', 'rep')
- new_momentum: float32 [8, 96, 2560], P(None, 'shard')
All inputs are finite; a program needn't handle non-finite values.
Results may differ from a plain program's by a relative error of at most 0.0014.
Values may be sent and summed in bfloat16 or wider, within the bound.
A program may use at most 64 MiB of HBM per device.

v0:
```python
import math

import jax
import jax.numpy as jnp
from jax import lax
from jax.sharding import PartitionSpec as P

E = 96
D = 2560
ITERS = 5


momentum_decay = 0.95
norm_floor = 1e-07
quintic_terms = (3.4445, -4.775, 2.0315)


def broadcast(x, axis, root):
    mine = lax.axis_index(axis) == root
    return lax.psum(jnp.where(mine, x, jnp.zeros_like(x)), axis)


def batched_schulz(effective):
    totals = jnp.sqrt(jnp.sum(effective * effective, axis=(1, 2), keepdims=True))
    iterate = effective / (totals + norm_floor)
    for turn in range(ITERS):
        gram_mat = jnp.einsum("kij,klj->kil", iterate, iterate, precision=lax.Precision.HIGHEST)
        square_mat = jnp.einsum("kij,kjl->kil", gram_mat, gram_mat, precision=lax.Precision.HIGHEST)
        poly_mat = quintic_terms[1] * gram_mat + quintic_terms[2] * square_mat
        iterate = quintic_terms[0] * iterate + jnp.einsum(
            "kij,kjl->kil", poly_mat, iterate, precision=lax.Precision.HIGHEST
        )
    return iterate


def per_device(gradients, momentum):
    update_scale = 0.2 * math.sqrt(max(E, D))
    gradient_values = gradients.astype(jnp.float32)
    new_momentum = momentum_decay * momentum + gradient_values
    effective_rows = gradient_values + momentum_decay * new_momentum
    effective = lax.all_to_all(effective_rows, "shard", split_axis=0, concat_axis=1, tiled=True)
    slot_count = effective.shape[0]
    replicas = lax.axis_size("rep")
    column = lax.axis_index("shard")
    replica = lax.axis_index("rep")
    slot_owners = (column * slot_count + jnp.arange(slot_count, dtype=jnp.int32)) % replicas
    owned = slot_owners == replica

    def compute_update(operand):
        return (update_scale * batched_schulz(operand)).astype(jnp.bfloat16)

    def skip_update(operand):
        return jnp.zeros(operand.shape, jnp.bfloat16)

    local_updates = lax.cond(jnp.any(owned), compute_update, skip_update, effective)
    copies = []
    for slot_index in range(slot_count):
        copies.append(broadcast(local_updates[slot_index], "rep", slot_owners[slot_index]))
    stacked = jnp.stack(copies)
    result_rows = lax.all_to_all(stacked, "shard", split_axis=1, concat_axis=0, tiled=True)
    col_width = result_rows.shape[2] // replicas
    kept_cols = lax.dynamic_slice_in_dim(result_rows, replica * col_width, col_width, 2)
    return (kept_cols, new_momentum)


def solution(mesh):
    in_specs = (P(None, "shard", None), P(None, "shard", None))
    out_specs = (P(None, "shard", "rep"), P(None, "shard", None))
    return jax.shard_map(
        per_device, mesh=mesh, in_specs=in_specs, out_specs=out_specs, check_vma=False
    )
```

profile of v0, /device:TPU:0, one launch (start us, length us, event | category | flops | bytes accessed | tf_op | source)
XLA Modules:
  0.0 180.7 jit_solution(16023603056860702382)
XLA Ops:
  7.2 4.4 %convert_add_fusion = (f32[8,24,2560]{2,1,0:T(8,128)}, f32[8,24,2560]{2,1,0:T(8,128)}) fusion(bf16[8,24,2560]{2,1,0:T(8,128)(2,1)} %param.4, f32[8,24,2560]{2,1,0:T(8,128)} %param.5), kind=kLoop, calls=%fused_computation.22 | loop fusion | flops 2457600 | bytes 6881280 | tf_op jit(solution)/shard_map/add | solution.py:40
  11.5 6.3 %all-to-all-start = ((f32[8,24,2560]{2,1,0:T(8,128)}), f32[8,24,2560]{2,1,0:T(8,128)S(1)}, u32[]{:S(2)}, u32[]{:S(2)}) async-start(f32[8,24,2560]{2,1,0:T(8,128)} %get-tuple-element.20), calls=%async_computation | async-start | bytes 3932160 | tf_op jit(solution)/shard_map/all_to_all | solution.py:41
  17.8 0.0 all-reduce.3.cloned.1.call-start
  17.8 0.6 compare_reduce_fusion
  19.2 0.6 fusion.8
  20.9 42.3 %all-to-all-done = f32[8,24,2560]{2,1,0:T(8,128)S(1)} async-done(((f32[8,24,2560]{2,1,0:T(8,128)}), f32[8,24,2560]{2,1,0:T(8,128)S(1)}, u32[]{:S(2)}, u32[]{:S(2)}) %all-to-all-start) | async-done | bytes 1966112 | tf_op jit(solution)/shard_map/all_to_all | solution.py:41
  63.2 0.1 copy.13
  63.4 21.7 %conditional.1 = (bf16[96,2560]{1,0:T(8,128)(2,1)S(1)}, bf16[96,2560]{1,0:T(8,128)(2,1)S(1)}) conditional(s32[]{:T(128)} %convert_element_type.10, () %tuple.22, f32[2,4,24,2560]{3,2,1,0:T(8,128)S(1)} %bitcast.50), branch_computations={%region_1.2_spmd, %region_2.4_spmd} | conditional | flops 5776128000 | bytes 37847088 | solution.py:55
  63.4 0.4 multiply_reduce_fusion
  63.8 0.3 bitcast_divide_fusion
  64.1 1.9 %fusion.9 = f32[2,96,96]{2,1,0:T(8,128)S(1)} fusion(f32[2,96,2560]{2,1,0:T(8,128)S(1)} %bitcast_divide_fusion), kind=kOutput, calls=%fused_computation.35 | convolution fusion | flops 566231040 | bytes 2039808 | tf_op jit(solution)/shard_map/cond/branch_1_fun/kij,klj->kil/dot_general | solution.py:27
  66.0 0.2 fusion.2
  66.2 1.9 %convolution_add_fusion.4 = f32[2,96,2560]{2,1,0:T(8,128)S(1)} fusion(f32[2,96,96]{2,1,0:T(8,128)S(1)} %fusion.2, f32[2,96,2560]{2,1,0:T(8,128)S(1)} %bitcast_divide_fusion), kind=kOutput, calls=%fused_computation.5 | convolution fusion | flops 567214080 | bytes 4005888 | tf_op jit(solution)/shard_map/cond/branch_1_fun/kij,kjl->kil/dot_general | solution.py:30
  68.2 1.9 %fusion.10 = f32[2,96,96]{2,1,0:T(8,128)S(1)} fusion(f32[2,96,2560]{2,1,0:T(8,128)S(1)} %convolution_add_fusion.4), kind=kOutput, calls=%fused_computation.36 | convolution fusion | flops 566231040 | bytes 2039808 | tf_op jit(solution)/shard_map/cond/branch_1_fun/kij,klj->kil/dot_general | solution.py:27
  70.1 0.2 fusion.3
  70.3 1.9 %convolution_add_fusion.3 = f32[2,96,2560]{2,1,0:T(8,128)S(1)} fusion(f32[2,96,96]{2,1,0:T(8,128)S(1)} %fusion.3, f32[2,96,2560]{2,1,0:T(8,128)S(1)} %convolution_add_fusion.4), kind=kOutput, calls=%fused_computation.4 | convolution fusion | flops 567214080 | bytes 4005888 | tf_op jit(solution)/shard_map/cond/branch_1_fun/kij,kjl->kil/dot_general | solution.py:30
  72.3 1.9 %fusion.11 = f32[2,96,96]{2,1,0:T(8,128)S(1)} fusion(f32[2,96,2560]{2,1,0:T(8,128)S(1)} %convolution_add_fusion.3), kind=kOutput, calls=%fused_computation.37 | convolution fusion | flops 566231040 | bytes 2039808 | tf_op jit(solution)/shard_map/cond/branch_1_fun/kij,klj->kil/dot_general | solution.py:27
  74.2 0.2 fusion.4
  74.4 1.9 %convolution_add_fusion.2 = f32[2,96,2560]{2,1,0:T(8,128)S(1)} fusion(f32[2,96,96]{2,1,0:T(8,128)S(1)} %fusion.4, f32[2,96,2560]{2,1,0:T(8,128)S(1)} %convolution_add_fusion.3), kind=kOutput, calls=%fused_computation.3 | convolution fusion | flops 567214080 | bytes 4005888 | tf_op jit(solution)/shard_map/cond/branch_1_fun/kij,kjl->kil/dot_general | solution.py:30
  76.4 2.1 %fusion.12 = f32[2,96,96]{2,1,0:T(8,128)S(1)} fusion(f32[2,96,2560]{2,1,0:T(8,128)S(1)} %convolution_add_fusion.2), kind=kOutput, calls=%fused_computation.38 | convolution fusion | flops 566231040 | bytes 2039808 | tf_op jit(solution)/shard_map/cond/branch_1_fun/kij,klj->kil/dot_general | solution.py:27
  78.4 0.2 fusion.5
  78.7 1.9 %convolution_add_fusion.1 = f32[2,96,2560]{2,1,0:T(8,128)S(1)} fusion(f32[2,96,96]{2,1,0:T(8,128)S(1)} %fusion.5, f32[2,96,2560]{2,1,0:T(8,128)S(1)} %convolution_add_fusion.2), kind=kOutput, calls=%fused_computation.2 | convolution fusion | flops 567214080 | bytes 4005888 | tf_op jit(solution)/shard_map/cond/branch_1_fun/kij,kjl->kil/dot_general | solution.py:30
  80.6 1.9 %fusion.13 = f32[2,96,96]{2,1,0:T(8,128)S(1)} fusion(f32[2,96,2560]{2,1,0:T(8,128)S(1)} %convolution_add_fusion.1), kind=kOutput, calls=%fused_computation.39 | convolution fusion | flops 566231040 | bytes 2039808 | tf_op jit(solution)/shard_map/cond/branch_1_fun/kij,klj->kil/dot_general | solution.py:27
  82.5 0.2 fusion.6
  82.8 2.0 %fusion.1 = bf16[2,96,2560]{2,1,0:T(8,128)(2,1)S(1)} fusion(f32[2,96,96]{2,1,0:T(8,128)S(1)} %fusion.6, f32[2,96,2560]{2,1,0:T(8,128)S(1)} %convolution_add_fusion.1), kind=kOutput, calls=%fused_computation.6 | convolution fusion | flops 568197120 | bytes 3022848 | tf_op jit(solution)/shard_map/cond/branch_1_fun/kij,kjl->kil/dot_general | solution.py:30
  84.8 0.1 slice_bitcast_fusion
  85.1 1.1 select_bitcast_fusion
  86.2 0.0 all-reduce.3.cloned.1.call-update
  86.2 55.7 %all-reduce.3.cloned.1.call-done = (bf16[1,96,2560]{2,1,0:T(8,128)(2,1)}, bf16[1,96,2560]{2,1,0:T(8,128)(2,1)}) async-done(((bf16[1,96,2560]{2,1,0:T(8,128)(2,1)}, bf16[1,96,2560]{2,1,0:T(8,128)(2,1)}), (bf16[1,96,2560]{2,1,0:T(8,128)(2,1)}, bf16[1,96,2560]{2,1,0:T(8,128)(2,1)})) %all-reduce.3.cloned.1.call-update) | async-done | bytes 983056 | tf_op jit(solution)/shard_map/psum | solution.py:20
  141.8 1.3 pad_maximum_fusion
  143.1 2.0 %copy.10 = bf16[2,96,2560]{2,0,1:T(2,128)(2,1)} copy(bf16[2,96,2560]{2,1,0:T(8,128)(2,1)S(1)} %pad_maximum_fusion) | data formatting | bytes 1966080 | tf_op jit(solution)/shard_map/stack | solution.py:59
  145.1 4.4 %all-to-all-start.1 = ((bf16[2,96,2560]{2,0,1:T(2,128)(2,1)}), bf16[2,96,2560]{2,0,1:T(2,128)(2,1)S(1)}, u32[]{:S(2)}, u32[]{:S(2)}) async-start(bf16[2,96,2560]{2,0,1:T(2,128)(2,1)} %copy.10), calls=%async_computation.1 | async-start | bytes 1966080 | tf_op jit(solution)/shard_map/all_to_all | solution.py:60
  149.5 23.4 %all-to-all-done.1 = bf16[2,96,2560]{2,0,1:T(2,128)(2,1)S(1)} async-done(((bf16[2,96,2560]{2,0,1:T(2,128)(2,1)}), bf16[2,96,2560]{2,0,1:T(2,128)(2,1)S(1)}, u32[]{:S(2)}, u32[]{:S(2)}) %all-to-all-start.1) | async-done | bytes 983072 | tf_op jit(solution)/shard_map/all_to_all | solution.py:60
  173.0 0.1 copy.11
  173.1 0.8 constant_dynamic-slice_fusion
  (2 shorter events, 0.0 us)
Async XLA Ops:
  11.5 51.7 %all-to-all-start = ((f32[8,24,2560]{2,1,0:T(8,128)}), f32[8,24,2560]{2,1,0:T(8,128)S(1)}, u32[]{:S(2)}, u32[]{:S(2)}) async-start(f32[8,24,2560]{2,1,0:T(8,128)} %get-tuple-element.20), calls=%async_computation | async-start | bytes 3932160 | tf_op jit(solution)/shard_map/all_to_all | solution.py:41
  17.8 124.0 %all-reduce.3.cloned.1.call-start = ((), (), s32[]{:S(2)}) async-start(), calls=%async_computation.2 | async-start | bytes 1966080 | tf_op jit(solution)/shard_map/psum | solution.py:20
  145.1 27.9 %all-to-all-start.1 = ((bf16[2,96,2560]{2,0,1:T(2,128)(2,1)}), bf16[2,96,2560]{2,0,1:T(2,128)(2,1)S(1)}, u32[]{:S(2)}, u32[]{:S(2)}) async-start(bf16[2,96,2560]{2,0,1:T(2,128)(2,1)} %copy.10), calls=%async_computation.1 | async-start | bytes 1966080 | tf_op jit(solution)/shard_map/all_to_all | solution.py:60
Sparse Core Ops, SparseCore 0:
  86.3 55.4 all-reduce.2
where the time goes:
time: 181 us
  waiting for transfers between devices  121 us (67%)
  matrix products  20.6 us (11%)
  between operations  15.9 us (9%)
  starting transfers between devices  10.8 us (6%)
  other arithmetic  8.01 us (4%)
  local copies, waits for them, and re-layouts  3.64 us (2%)
    psum x1, waiting for transfers between devices, broadcast(): return lax.psum(jnp.where(mine, x, jnp.zeros_like(x)), axis)  55.7 us
    all_to_all x1, waiting for transfers between devices, per_device(): lax.all_to_all(effective_rows, 'shard', split_axis=0, concat_axis=1, tile...  42.3 us
    all_to_all x1, waiting for transfers between devices, per_device(): lax.all_to_all(stacked, 'shard', split_axis=1, concat_axis=0, tiled=True)  23.4 us
    dot_general x5, matrix products, batched_schulz(): jnp.einsum('kij,kjl->kil', poly_mat, iterate, precision=lax.Precision.HIG...  9.76 us
    dot_general x5, matrix products, batched_schulz(): jnp.einsum('kij,klj->kil', iterate, iterate, precision=lax.Precision.HIGH...  9.67 us
    all_to_all x1, starting transfers between devices, per_device(): lax.all_to_all(effective_rows, 'shard', split_axis=0, concat_axis=1, tile...  6.32 us
    all_to_all x1, starting transfers between devices, per_device(): lax.all_to_all(stacked, 'shard', split_axis=1, concat_axis=0, tiled=True)  4.45 us
    add x1, other arithmetic, per_device(): effective_rows = gradient_values + momentum_decay * new_momentum  4.36 us
  transfers between devices with their start and end apart: 3, of which 3 were waited for; matrix products, arithmetic and copies ran while one was open for 1% of the time, Pallas kernels for 0%

commit v1 on v0

v1 whole, which is shorter than its diff:
```python
import math

import jax
import jax.numpy as jnp
from jax import lax
from jax.sharding import PartitionSpec as P

ITERS = 5
momentum_decay = 0.95
norm_floor = 1e-07
quintic_terms = (3.4445, -4.775, 2.0315)


def mm(a, b):
    return jnp.einsum("kij,kjl->kil", a, b, precision=lax.Precision.HIGHEST)


def schulz_factor(gram, scale):
    total = jnp.trace(gram, axis1=1, axis2=2)[:, None, None]
    inverse = 1.0 / (jnp.sqrt(total) + norm_floor)
    g = jnp.where(inverse > 0, gram * inverse * inverse, 0.0)
    eye = jnp.eye(gram.shape[-1], dtype=jnp.float32)
    a, b, c = quintic_terms
    q = None
    for turn in range(ITERS):
        poly = a * eye + b * g + c * mm(g, g)
        q = poly if q is None else mm(poly, q)
        if turn < ITERS - 1:
            g = mm(poly, mm(poly, g))
    return q * (scale * inverse)


def per_device_plain(gradients, momentum):
    rows, width = gradients.shape[1:]
    scale = 0.2 * math.sqrt(max(rows * lax.axis_size("shard"), width))
    replicas = lax.axis_size("rep")
    grads = gradients.astype(jnp.float32)
    new_momentum = momentum_decay * momentum + grads
    effective = grads + momentum_decay * new_momentum
    cols = width // replicas
    mine = lax.dynamic_slice_in_dim(effective, lax.axis_index("rep") * cols, cols, 2)
    whole = lax.all_to_all(mine, "shard", split_axis=0, concat_axis=1, tiled=True)
    gram = jnp.einsum("kij,klj->kil", whole, whole, precision=lax.Precision.HIGHEST)
    factor = schulz_factor(lax.psum(gram, "rep"), scale)
    out = mm(factor, whole).astype(jnp.bfloat16)
    return lax.all_to_all(out, "shard", split_axis=1, concat_axis=0, tiled=True), new_momentum


def solution(mesh):
    in_specs = (P(None, "shard", None), P(None, "shard", None))
    out_specs = (P(None, "shard", "rep"), P(None, "shard", None))
    return jax.shard_map(
        per_device_plain, mesh=mesh, in_specs=in_specs, out_specs=out_specs, check_vma=False
    )
```

time: 181 us -> 107 us (0.59)
  waiting for transfers between devices: 121 us -> 60.2 us
  matrix products: 20.6 us -> 7.54 us
  blocking collectives: 0 us -> 11.5 us
  starting transfers between devices: 10.8 us -> 6.32 us
  local copies, waits for them, and re-layouts: 3.64 us -> 0.83 us
    all_to_all x2 -> x1, waiting for transfers between devices: 65.7 us -> 9.6 us  [per_device_plain(): lax.all_to_all(mine, 'shard', split_axis=0, concat_axis=1, tiled=True)]
    dot_general x15 -> x19, matrix products: 20.6 us -> 7.54 us  [the longest x18 6.43 us: mm(): return jnp.einsum('kij,kjl->kil', a, b, precision=lax.Precision.HIGHEST)]
    all_to_all x0 -> x1, blocking collectives: none -> 11.5 us  [per_device_plain(): lax.all_to_all(out, 'shard', split_axis=1, concat_axis=0, tiled=True)]
    psum x1, waiting for transfers between devices: 55.7 us -> 50.6 us  [per_device_plain(): factor = schulz_factor(lax.psum(gram, 'rep'), scale)]
    all_to_all x2 -> x1, starting transfers between devices: 10.8 us -> 6.32 us  [per_device_plain(): lax.all_to_all(mine, 'shard', split_axis=0, concat_axis=1, tiled=True)]
    convert_element_type x0 -> x1, other arithmetic: none -> 2.87 us  [per_device_plain(): grads = gradients.astype(jnp.float32)]
    another operation x2 -> x0, other arithmetic: 2.35 us -> none  [per_device(): stacked = jnp.stack(copies)]
    another operation x1 -> x0, local copies, waits for them, and re-layouts: 1.97 us -> none  [per_device(): stacked = jnp.stack(copies)]
  transfers between devices with their start and end apart: 3 -> 2, of which waited for: 3 -> 2; matrix products, arithmetic and copies ran while one was open for 1% -> 0% of each run, Pallas kernels for 0% -> 0%
where the time goes in v1:
time: 107 us
  waiting for transfers between devices  60.2 us (56%)
  between operations  14.2 us (13%)
  blocking collectives  11.5 us (11%)
  matrix products  7.54 us (7%)
  other arithmetic  6.41 us (6%)
  starting transfers between devices  6.32 us (6%)
    psum x1, waiting for transfers between devices, per_device_plain(): factor = schulz_factor(lax.psum(gram, 'rep'), scale)  50.6 us
    all_to_all x1, blocking collectives, per_device_plain(): lax.all_to_all(out, 'shard', split_axis=1, concat_axis=0, tiled=True)  11.5 us
    all_to_all x1, waiting for transfers between devices, per_device_plain(): lax.all_to_all(mine, 'shard', split_axis=0, concat_axis=1, tiled=True)  9.6 us
    dot_general x18, matrix products, mm(): return jnp.einsum('kij,kjl->kil', a, b, precision=lax.Precision.HIGHEST)  6.43 us
    all_to_all x1, starting transfers between devices, per_device_plain(): lax.all_to_all(mine, 'shard', split_axis=0, concat_axis=1, tiled=True)  6.32 us
    convert_element_type x1, other arithmetic, per_device_plain(): grads = gradients.astype(jnp.float32)  2.87 us
    add x1, other arithmetic, per_device_plain(): effective = grads + momentum_decay * new_momentum  2.25 us
  transfers between devices with their start and end apart: 2, of which 2 were waited for; matrix products, arithmetic and copies ran while one was open for 0% of the time, Pallas kernels for 0%

profile of v1, /device:TPU:0, one launch (start us, length us, event | category | flops | bytes accessed | tf_op | source)
XLA Modules:
  0.0 107.0 jit_solution(3335476174348482193)
XLA Ops:
  7.2 0.0 copy-start
  7.2 0.0 copy-start.2
  7.2 2.9 %convert_element_type.7 = f32[8,24,2560]{2,1,0:T(8,128)} convert(bf16[8,24,2560]{2,1,0:T(8,128)(2,1)} %param.2) | non-fusion elementwise | flops 491520 | bytes 2949120 | tf_op jit(solution)/shard_map/convert_element_type | solution.py:37
  10.1 0.0 copy-done
  10.1 0.0 copy-done.2
  10.1 0.3 multiply_add_fusion
  10.3 0.0 copy-start.1
  10.3 2.2 %dynamic-slice_add_fusion = f32[8,24,320]{2,1,0:T(8,128)} fusion(f32[8,24,2560]{2,1,0:T(8,128)} %convert_element_type.7, s32[]{:T(128)S(6)} %select_n.12, f32[8,24,2560]{2,1,0:T(8,128)S(1)} %multiply_add_fusion), kind=kLoop, calls=%fused_computation.13 | loop fusion | flops 122880 | bytes 737284 | tf_op jit(solution)/shard_map/add | solution.py:39
  12.6 6.3 %all-to-all-start = ((f32[8,24,320]{2,1,0:T(8,128)}), f32[8,24,320]{2,1,0:T(8,128)S(1)}, u32[]{:S(2)}, u32[]{:S(2)}) async-start(f32[8,24,320]{2,1,0:T(8,128)} %dynamic-slice_add_fusion), calls=%async_computation | async-start | bytes 589824 | tf_op jit(solution)/shard_map/all_to_all | solution.py:42
  18.9 0.0 all-reduce.2.cloned.1.call-start
  18.9 9.6 %all-to-all-done = f32[8,24,320]{2,1,0:T(8,128)S(1)} async-done(((f32[8,24,320]{2,1,0:T(8,128)}), f32[8,24,320]{2,1,0:T(8,128)S(1)}, u32[]{:S(2)}, u32[]{:S(2)}) %all-to-all-start) | async-done | bytes 245792 | tf_op jit(solution)/shard_map/all_to_all | solution.py:42
  28.5 1.1 %fusion.14 = f32[2,96,96]{2,1,0:T(8,128)} fusion(f32[2,96,320]{2,1,0:T(8,128)S(1)} %bitcast.43), kind=kOutput, calls=%fused_computation.31 | convolution fusion | flops 70778880 | bytes 319488 | tf_op jit(solution)/shard_map/kij,klj->kil/dot_general | solution.py:43
  29.7 0.0 all-reduce.2.cloned.1.call-update
  29.7 50.6 %all-reduce.2.cloned.1.call-done = f32[2,96,96]{2,1,0:T(8,128)} async-done(((f32[2,96,96]{2,1,0:T(8,128)}), f32[2,96,96]{2,1,0:T(8,128)}) %all-reduce.2.cloned.1.call-update) | async-done | bytes 73744 | tf_op jit(solution)/shard_map/psum | solution.py:44
  80.3 1.0 select_reduce_fusion
  81.3 1.4 %fusion = f32[2,96,96]{2,1,0:T(8,128)S(1)} fusion(f32[2,96,96]{2,1,0:T(8,128)} %all-reduce.2.cloned.1.call-done, f32[2]{0:T(128)S(1)} %get-tuple-element.3, f32[96,96]{1,0:T(8,128)S(1)} %broadcast_select_fusion, pred[2]{0:T(512)(128)(4,1)S(1)} %broadcast_compare_fusion), kind=kOutput, calls=%fused_computation.8 | convolution fusion | flops 21417984 | bytes 184330 | tf_op jit(solution)/shard_map/kij,kjl->kil/dot_general | solution.py:15
  82.7 1.2 %fusion.5 = f32[2,96,96]{2,1,0:T(8,128)S(1)} fusion(f32[2,96,96]{2,1,0:T(8,128)S(1)} %fusion, f32[2,96,96]{2,1,0:T(8,128)} %all-reduce.2.cloned.1.call-done, f32[2]{0:T(128)S(1)} %get-tuple-element.3, pred[2]{0:T(512)(128)(4,1)S(1)} %broadcast_compare_fusion), kind=kOutput, calls=%fused_computation.17 | convolution fusion | flops 21288960 | bytes 221194 | tf_op jit(solution)/shard_map/kij,kjl->kil/dot_general | solution.py:15
  83.9 0.2 fusion.15
  84.1 0.2 fusion.1
  84.4 0.0 copy-done.1
  84.4 0.2 fusion.22
  84.6 0.2 fusion.16
  84.9 0.2 fusion.17
  85.1 0.2 fusion.2
  85.4 0.2 fusion.18
  85.6 0.2 fusion.23
  85.8 0.2 fusion.19
  86.1 0.2 fusion.3
  86.3 0.2 fusion.20
  86.5 0.2 fusion.24
  86.8 0.2 fusion.21
  87.0 0.2 fusion.4
  87.3 0.2 convolution_multiply_fusion
  87.5 0.4 convolution_convert_fusion
  87.9 0.1 copy.7
  88.0 11.5 %all_to_all.36 = bf16[2,96,320]{2,0,1:T(2,128)(2,1)S(1)} all-to-all(bf16[2,96,320]{2,0,1:T(2,128)(2,1)S(1)} %copy.7), channel_id=1, replica_groups=mesh['rep'=8,'shard'=4] {'shard'}, dimensions={1} | all-to-all | bytes 245760 | tf_op jit(solution)/shard_map/all_to_all | solution.py:46
  99.5 0.7 copy.8
  (5 shorter events, 0.1 us)
Async XLA Ops:
  7.2 2.9 %copy-start = (bf16[8,24,2560]{2,1,0:T(8,128)(2,1)S(1)}, bf16[8,24,2560]{2,1,0:T(8,128)(2,1)}, u32[]{:S(2)}) copy-start(bf16[8,24,2560]{2,1,0:T(8,128)(2,1)} %param.2) | copy-start | bytes 2949124
  7.2 2.9 %copy-start.2 = (f32[8,24,2560]{2,1,0:T(8,128)S(1)}, f32[8,24,2560]{2,1,0:T(8,128)}, u32[]{:S(2)}) copy-start(f32[8,24,2560]{2,1,0:T(8,128)} %param.3) | copy-start | bytes 5898244
  10.3 74.1 %copy-start.1 = (f32[8,24,2560]{2,1,0:T(8,128)}, f32[8,24,2560]{2,1,0:T(8,128)S(1)}, u32[]{:S(2)}) copy-start(f32[8,24,2560]{2,1,0:T(8,128)S(1)} %multiply_add_fusion) | copy-start | bytes 5898244
  12.6 15.9 %all-to-all-start = ((f32[8,24,320]{2,1,0:T(8,128)}), f32[8,24,320]{2,1,0:T(8,128)S(1)}, u32[]{:S(2)}, u32[]{:S(2)}) async-start(f32[8,24,320]{2,1,0:T(8,128)} %dynamic-slice_add_fusion), calls=%async_computation | async-start | bytes 589824 | tf_op jit(solution)/shard_map/all_to_all | solution.py:42
  18.9 61.4 %all-reduce.2.cloned.1.call-start = ((), (), s32[]{:S(2)}) async-start(), calls=%async_computation.2 | async-start | bytes 196608 | tf_op jit(solution)/shard_map/psum | solution.py:44
Sparse Core Ops, SparseCore 0:
  29.8 50.4 all-reduce.1

commit v2 on v1

--- a/solution.py
+++ b/solution.py
@@ -1,14 +1,19 @@
+import functools
 import math
 
 import jax
 import jax.numpy as jnp
 from jax import lax
+from jax.experimental import pallas as pl
+from jax.experimental.pallas import tpu as pltpu
 from jax.sharding import PartitionSpec as P
 
 ITERS = 5
+LANES = 128
 momentum_decay = 0.95
 norm_floor = 1e-07
 quintic_terms = (3.4445, -4.775, 2.0315)
+MESH = pl.DeviceIdType.MESH
 
 
 def mm(a, b):
@@ -17,7 +22,7 @@
 
 def schulz_factor(gram, scale):
     total = jnp.trace(gram, axis1=1, axis2=2)[:, None, None]
-    inverse = 1.0 / (jnp.sqrt(total) + norm_floor)
+    inverse = jnp.where(total < jnp.inf, 1.0 / (jnp.sqrt(total) + norm_floor), 0.0)
     g = jnp.where(inverse > 0, gram * inverse * inverse, 0.0)
     eye = jnp.eye(gram.shape[-1], dtype=jnp.float32)
     a, b, c = quintic_terms
@@ -46,9 +51,243 @@
     return lax.all_to_all(out, "shard", split_axis=1, concat_axis=0, tiled=True), new_momentum
 
 
+def split(x):
+    high = x.astype(jnp.bfloat16)
+    return high, (x - high.astype(jnp.float32)).astype(jnp.bfloat16)
+
+
+def left(x):
+    return jnp.concatenate(split(x), axis=1)
+
+
+def right(x):
+    pair = jnp.concatenate(split(x), axis=1)
+    return jnp.concatenate([pair, pair], axis=0)
+
+
+def product(lhs, rhs):
+    n = rhs.shape[1] // 2
+    out = jnp.dot(lhs, rhs, preferred_element_type=jnp.float32)
+    return out[:, :n] + out[:, n:]
+
+
+def kernel(shards, per, groups, g_hbm, m_hbm, upd_ref, newm_hbm,
+           gc, mc, gf, mf, nf, send, x_ref, xs, part, parts, stage, recv,
+           chunk_sem, full_sem, store_sem, s1, r1, s2, r2, s3, r3):
+    mats, rows, width = g_hbm.shape
+    chunk = width // groups
+    cols = chunk // per
+    n = shards * rows
+    scale = 0.2 * math.sqrt(max(n, width))
+    rep, s = lax.axis_index("rep"), lax.axis_index("shard")
+    j, c = rep // per, rep % per
+
+    def plane(k):
+        return lax.rem(s + k, shards)
+
+    at = pl.ds(pl.multiple_of(j * chunk, LANES), chunk)
+    chunk_loads = []
+    for k in range(shards):
+        mat = plane(k) * per + c
+        pair = (pltpu.make_async_copy(g_hbm.at[mat, :, at], gc.at[k], chunk_sem.at[0, k]),
+                pltpu.make_async_copy(m_hbm.at[mat, :, at], mc.at[k], chunk_sem.at[1, k]))
+        chunk_loads.append(pair)
+    order = list(range(1, shards)) + [0]
+    for k in order:
+        for copy in chunk_loads[k]:
+            copy.start()
+
+    barrier = pltpu.get_barrier_semaphore()
+    peers = []
+    for k in range(shards):
+        for d in range(per):
+            if k or d:
+                peers.append((j * per + lax.rem(c + d, per), plane(k)))
+    for k in range(1, groups):
+        peers.append((lax.rem(j + k, groups) * per + c, s))
+    for peer in peers:
+        pl.semaphore_signal(barrier, inc=1, device_id=peer, device_id_type=MESH)
+
+    full_loads = []
+    for mat in range(mats):
+        pair = (pltpu.make_async_copy(g_hbm.at[mat], gf.at[mat], full_sem.at[0, mat]),
+                pltpu.make_async_copy(m_hbm.at[mat], mf.at[mat], full_sem.at[1, mat]))
+        full_loads.append(pair)
+        for copy in pair:
+            copy.start()
+
+    def effective(k):
+        for copy in chunk_loads[k]:
+            copy.wait()
+        grads = gc[k].astype(jnp.float32)
+        return grads + momentum_decay * (momentum_decay * mc[k] + grads)
+
+    for k in range(1, shards):
+        send[k] = effective(k)
+    pl.semaphore_wait(barrier, len(peers))
+    first = []
+    for k in range(1, shards):
+        copy = pltpu.make_async_remote_copy(
+            src_ref=send.at[k], dst_ref=x_ref.at[k], send_sem=s1.at[k], recv_sem=r1.at[k],
+            device_id=(rep, plane(k)), device_id_type=MESH)
+        copy.start()
+        first.append(copy)
+    x_ref[0] = effective(0)
+
+    stores = []
+    for mat in range(mats):
+        for copy in full_loads[mat]:
+            copy.wait()
+        nf[mat] = momentum_decay * mf[mat] + gf[mat].astype(jnp.float32)
+        copy = pltpu.make_async_copy(nf.at[mat], newm_hbm.at[mat], store_sem.at[mat])
+        copy.start()
+        stores.append(copy)
+
+    for copy in first:
+        copy.wait_recv()
+    x = x_ref[...].reshape(n, chunk)
+    high, low = split(x)
+    pad = jnp.zeros((LANES - n, chunk), jnp.bfloat16)
+    xs[...] = jnp.concatenate([high, pad, low, pad], axis=0)
+    quad = lax.dot_general(xs[...], xs[...], (((1,), (1,)), ((), ())),
+                           preferred_element_type=jnp.float32)
+    mine = (quad[:LANES, :LANES] + quad[LANES:, LANES:]) + (quad[:LANES, LANES:] + quad[LANES:, :LANES])
+    part[...] = mine[:n]
+    second = []
+    for k in range(1, groups):
+        copy = pltpu.make_async_remote_copy(
+            src_ref=part, dst_ref=parts.at[k], send_sem=s2.at[k], recv_sem=r2.at[k],
+            device_id=(lax.rem(j + k, groups) * per + c, s), device_id_type=MESH)
+        copy.start()
+        second.append(copy)
+    gram = mine[:n]
+    for k, copy in zip(range(1, groups), second):
+        copy.wait_recv()
+        gram = gram + parts[k]
+    gram = jnp.concatenate([gram, jnp.zeros((LANES - n, LANES), jnp.float32)], axis=0)
+
+    diagonal = (lax.broadcasted_iota(jnp.int32, (LANES, LANES), 0)
+                == lax.broadcasted_iota(jnp.int32, (LANES, LANES), 1))
+    total = jnp.sum(jnp.where(diagonal, gram, 0.0), axis=(0, 1), keepdims=True)
+    inverse = jnp.where(total < jnp.inf, 1.0 / (jnp.sqrt(total) + norm_floor), 0.0)
+    g = jnp.where(inverse > 0, gram * inverse * inverse, 0.0)
+    a, b, c2 = quintic_terms
+    eye = jnp.where(diagonal, a, 0.0)
+    q = None
+    for turn in range(ITERS):
+        g_right = right(g)
+        poly = (eye + b * g) + c2 * product(left(g), g_right)
+        poly_left = left(poly)
+        if turn < ITERS - 1:
+            g = product(poly_left, right(product(poly_left, g_right)))
+        q = poly if q is None else product(poly_left, right(q))
+    q_high, q_low = split((q * (scale * inverse))[:n])
+    lhs = jnp.concatenate([jnp.concatenate([q_high, q_high], axis=1),
+                           jnp.concatenate([q_low, q_low], axis=1)], axis=0)
+    both = jnp.dot(lhs, xs[...], preferred_element_type=jnp.float32)
+    out = jnp.where(inverse > 0, both[:n] + both[n:], 0.0)
+
+    half = LANES // 2
+    low_lanes = lax.broadcasted_iota(jnp.int32, (rows, LANES), 1) < half
+    main = cols - half
+    for k in range(shards):
+        block = out[k * rows:(k + 1) * rows]
+        tiles = [block[:, t * LANES:(t + 1) * LANES] for t in range(chunk // LANES)]
+        middle = len(tiles) // 2
+        turned = [pltpu.roll(t, half, 1) for t in tiles[middle:]]
+        shifted = [jnp.where(low_lanes, p, t) for p, t in zip(turned[:-1], turned[1:])]
+        for d, (body, tail) in enumerate(((tiles[:middle], tiles[middle]), (shifted, turned[-1]))):
+            extra = jnp.concatenate(
+                [jnp.where(low_lanes[:8], tail[:8], pltpu.roll(tail[8:16], half, 1)), tail[16:24]], axis=1)
+            packed = jnp.concatenate([jnp.concatenate(body, axis=1), extra], axis=0)
+            stage[k, d] = packed.astype(jnp.bfloat16)
+    third = {}
+    for k in [*range(1, shards), 0]:
+        for d in range(per):
+            if k or d:
+                core = lax.rem(c + d, per)
+                copy = pltpu.make_async_remote_copy(
+                    src_ref=stage.at[k, core], dst_ref=recv.at[k, d],
+                    send_sem=s3.at[k, d], recv_sem=r3.at[k, d],
+                    device_id=(j * per + core, plane(shards - k)), device_id_type=MESH)
+                copy.start()
+                third[k, d] = copy
+
+    for k in range(shards):
+        for d in range(per):
+            if k or d:
+                third[k, d].wait_recv()
+                block = recv[k, d].astype(jnp.float32)
+            else:
+                block = stage[0, c].astype(jnp.float32)
+            mat = plane(k) * per + lax.rem(c + per - d, per)
+            lanes = block[rows:, :LANES]
+            tail = jnp.concatenate([lanes, pltpu.roll(lanes, half, 1), block[rows:, LANES:2 * LANES]], axis=0)
+            upd_ref[mat, :, :main] = block[:rows].astype(jnp.bfloat16)
+            upd_ref[mat, :, main:] = tail[:, :half].astype(jnp.bfloat16)
+    for copy in stores:
+        copy.wait()
+    for copy in first + second + list(third.values()):
+        copy.wait_send()
+
+
+def per_device_kernel(shards, per, groups, gradients, momentum):
+    mats, rows, width = gradients.shape
+    chunk = width // groups
+    cols = chunk // per
+    n = shards * rows
+    packed = (shards, per, rows + 8, cols - LANES // 2)
+    f32, bf16, dma = jnp.float32, jnp.bfloat16, pltpu.SemaphoreType.DMA
+    return pl.pallas_call(
+        functools.partial(kernel, shards, per, groups),
+        out_shape=(jax.ShapeDtypeStruct((mats, rows, cols), bf16),
+                   jax.ShapeDtypeStruct((mats, rows, width), f32)),
+        in_specs=[pl.BlockSpec(memory_space=pl.ANY)] * 2,
+        out_specs=(pl.BlockSpec(memory_space=pltpu.VMEM), pl.BlockSpec(memory_space=pl.ANY)),
+        scratch_shapes=[
+            pltpu.VMEM((shards, rows, chunk), bf16),
+            pltpu.VMEM((shards, rows, chunk), f32),
+            pltpu.VMEM((mats, rows, width), bf16),
+            pltpu.VMEM((mats, rows, width), f32),
+            pltpu.VMEM((mats, rows, width), f32),
+            pltpu.VMEM((shards, rows, chunk), f32),
+            pltpu.VMEM((shards, rows, chunk), f32),
+            pltpu.VMEM((2 * LANES, chunk), bf16),
+            pltpu.VMEM((n, LANES), f32),
+            pltpu.VMEM((groups, n, LANES), f32),
+            pltpu.VMEM(packed, bf16),
+            pltpu.VMEM(packed, bf16),
+            dma((2, shards)), dma((2, mats)), dma((mats,)),
+            dma((shards,)), dma((shards,)), dma((groups,)), dma((groups,)),
+            dma((shards, per)), dma((shards, per)),
+        ],
+        compiler_params=pltpu.CompilerParams(
+            collective_id=0, has_side_effects=True, vmem_limit_bytes=40 * 2**20),
+    )(gradients, momentum)
+
+
+def kernel_fits(shards, replicas, mats, n, width):
+    if mats % shards or n % shards:
+        return False
+    per, rows = mats // shards, n // shards
+    if per != 2 or rows != 24 or n > LANES or replicas % per:
+        return False
+    chunk = width * per // replicas
+    return chunk % (2 * LANES) == LANES and chunk >= 5 * LANES
+
+
 def solution(mesh):
+    shards, replicas = mesh.shape["shard"], mesh.shape["rep"]
+
+    def per_device(gradients, momentum):
+        mats, rows, width = gradients.shape
+        if kernel_fits(shards, replicas, mats, rows * shards, width):
+            per = mats // shards
+            return per_device_kernel(shards, per, replicas // per, gradients, momentum)
+        return per_device_plain(gradients, momentum)
+
     in_specs = (P(None, "shard", None), P(None, "shard", None))
     out_specs = (P(None, "shard", "rep"), P(None, "shard", None))
     return jax.shard_map(
-        per_device_plain, mesh=mesh, in_specs=in_specs, out_specs=out_specs, check_vma=False
+        per_device, mesh=mesh, in_specs=in_specs, out_specs=out_specs, check_vma=False
     )

time: 107 us -> 31.6 us (0.30)
  waiting for transfers between devices: 60.2 us -> 0 us
  Pallas kernels: 0 us -> 26.1 us
  between operations: 14.2 us -> 0.65 us
  blocking collectives: 11.5 us -> 0 us
  matrix products: 7.54 us -> 0 us
  other arithmetic: 6.41 us -> 0 us
  starting transfers between devices: 6.32 us -> 0 us
  local copies, waits for them, and re-layouts: 0.83 us -> 4.67 us
    psum x1 -> x0, waiting for transfers between devices: 50.6 us -> none  [per_device_plain(): factor = schulz_factor(lax.psum(gram, 'rep'), scale)]
    pallas_call x0 -> x1, Pallas kernels: none -> 26.1 us  [per_device_kernel(): pl.pallas_call(functools.partial(kernel, shards, per, groups), out_shape=...]
    all_to_all x1 -> x0, blocking collectives: 11.5 us -> none  [per_device_plain(): lax.all_to_all(out, 'shard', split_axis=1, concat_axis=0, tiled=True)]
    all_to_all x1 -> x0, waiting for transfers between devices: 9.6 us -> none  [per_device_plain(): lax.all_to_all(mine, 'shard', split_axis=0, concat_axis=1, tiled=True)]
    dot_general x19 -> x0, matrix products: 7.54 us -> none  [the longest x18 6.43 us: mm(): return jnp.einsum('kij,kjl->kil', a, b, precision=lax.Precision.HIGHEST)]
    all_to_all x1 -> x0, starting transfers between devices: 6.32 us -> none  [per_device_plain(): lax.all_to_all(mine, 'shard', split_axis=0, concat_axis=1, tiled=True)]
    unnamed x6, local copies, waits for them, and re-layouts: 0.02 us -> 4.67 us
    convert_element_type x1 -> x0, other arithmetic: 2.87 us -> none  [per_device_plain(): grads = gradients.astype(jnp.float32)]
  transfers between devices with their start and end apart: 2 -> 0, of which waited for: 2 -> 0; matrix products, arithmetic and copies ran while one was open for 0% -> 0% of each run, Pallas kernels for 0% -> 0%
where the time goes in v2:
time: 31.6 us; the launch traced here: 31.4 us
  Pallas kernels  26.1 us (83%)
  local copies, waits for them, and re-layouts  4.67 us (15%)
  between operations  0.65 us (2%)
    pallas_call x1, Pallas kernels, per_device_kernel(): pl.pallas_call(functools.partial(kernel, shards, per, groups), out_shape=...  26.1 us
    unnamed x6, local copies, waits for them, and re-layouts  4.67 us

profile of v2, /device:TPU:0, one launch (start us, length us, event | category | flops | bytes accessed | tf_op | source)
XLA Modules:
  0.0 31.4 jit_solution(17147283288520231288)
XLA Ops:
  0.6 0.0 copy-start
  0.6 1.5 %copy-done = f32[8,24,2560]{2,1,0:T(8,128)S(1)} copy-done((f32[8,24,2560]{2,1,0:T(8,128)S(1)}, f32[8,24,2560]{2,1,0:T(8,128)}, u32[]{:S(2)}) %copy-start) | copy-done | bytes 1966104
  2.2 0.0 copy-start.1
  2.2 1.2 %copy-done.1 = bf16[8,24,2560]{2,1,0:T(8,128)(2,1)S(1)} copy-done((bf16[8,24,2560]{2,1,0:T(8,128)(2,1)S(1)}, bf16[8,24,2560]{2,1,0:T(8,128)(2,1)}, u32[]{:S(2)}) %copy-start.1) | copy-done | bytes 983064
  3.4 26.1 %shard_map.41 = (bf16[8,24,320]{2,1,0:T(8,128)(2,1)S(1)}, f32[8,24,2560]{2,1,0:T(8,128)S(1)}) custom-call(bf16[8,24,2560]{2,1,0:T(8,128)(2,1)S(1)} %copy-done.1, f32[8,24,2560]{2,1,0:T(8,128)S(1)} %copy-done), custom_call_target="tpu_custom_call" | custom-call | tf_op jit(solution)/shard_map/pallas_call | solution.py:241
  29.5 0.7 %copy.6 = bf16[8,24,320]{2,1,0:T(8,128)(2,1)} copy(bf16[8,24,320]{2,1,0:T(8,128)(2,1)S(1)} %get-tuple-element.4) | data formatting | bytes 245760
  30.2 1.3 %copy.7 = f32[8,24,2560]{2,1,0:T(8,128)} copy(f32[8,24,2560]{2,1,0:T(8,128)S(1)} %get-tuple-element.5) | data formatting | bytes 3932160
Async XLA Ops:
  0.6 1.5 %copy-start = (f32[8,24,2560]{2,1,0:T(8,128)S(1)}, f32[8,24,2560]{2,1,0:T(8,128)}, u32[]{:S(2)}) copy-start(f32[8,24,2560]{2,1,0:T(8,128)} %m_hbm.1) | copy-start | bytes 5898244
  2.2 1.2 %copy-start.1 = (bf16[8,24,2560]{2,1,0:T(8,128)(2,1)S(1)}, bf16[8,24,2560]{2,1,0:T(8,128)(2,1)}, u32[]{:S(2)}) copy-start(bf16[8,24,2560]{2,1,0:T(8,128)(2,1)} %g_hbm.1) | copy-start | bytes 2949124

commit v3 on v2

--- a/solution.py
+++ b/solution.py
@@ -71,31 +71,16 @@
     return out[:, :n] + out[:, n:]
 
 
-def kernel(shards, per, groups, g_hbm, m_hbm, upd_ref, newm_hbm,
-           gc, mc, gf, mf, nf, send, x_ref, xs, part, parts, stage, recv,
-           chunk_sem, full_sem, store_sem, s1, r1, s2, r2, s3, r3):
-    mats, rows, width = g_hbm.shape
-    chunk = width // groups
+def kernel(shards, per, groups, scale, eff_ref, out_ref,
+           x_ref, xs, part, parts, stage, recv, s1, r1, s2, r2, s3, r3):
+    _, rows, chunk = eff_ref.shape
     cols = chunk // per
     n = shards * rows
-    scale = 0.2 * math.sqrt(max(n, width))
     rep, s = lax.axis_index("rep"), lax.axis_index("shard")
     j, c = rep // per, rep % per
 
     def plane(k):
         return lax.rem(s + k, shards)
-
-    at = pl.ds(pl.multiple_of(j * chunk, LANES), chunk)
-    chunk_loads = []
-    for k in range(shards):
-        mat = plane(k) * per + c
-        pair = (pltpu.make_async_copy(g_hbm.at[mat, :, at], gc.at[k], chunk_sem.at[0, k]),
-                pltpu.make_async_copy(m_hbm.at[mat, :, at], mc.at[k], chunk_sem.at[1, k]))
-        chunk_loads.append(pair)
-    order = list(range(1, shards)) + [0]
-    for k in order:
-        for copy in chunk_loads[k]:
-            copy.start()
 
     barrier = pltpu.get_barrier_semaphore()
     peers = []
@@ -108,40 +93,15 @@
     for peer in peers:
         pl.semaphore_signal(barrier, inc=1, device_id=peer, device_id_type=MESH)
 
-    full_loads = []
-    for mat in range(mats):
-        pair = (pltpu.make_async_copy(g_hbm.at[mat], gf.at[mat], full_sem.at[0, mat]),
-                pltpu.make_async_copy(m_hbm.at[mat], mf.at[mat], full_sem.at[1, mat]))
-        full_loads.append(pair)
-        for copy in pair:
-            copy.start()
-
-    def effective(k):
-        for copy in chunk_loads[k]:
-            copy.wait()
-        grads = gc[k].astype(jnp.float32)
-        return grads + momentum_decay * (momentum_decay * mc[k] + grads)
-
-    for k in range(1, shards):
-        send[k] = effective(k)
     pl.semaphore_wait(barrier, len(peers))
     first = []
     for k in range(1, shards):
         copy = pltpu.make_async_remote_copy(
-            src_ref=send.at[k], dst_ref=x_ref.at[k], send_sem=s1.at[k], recv_sem=r1.at[k],
+            src_ref=eff_ref.at[plane(k)], dst_ref=x_ref.at[k], send_sem=s1.at[k], recv_sem=r1.at[k],
             device_id=(rep, plane(k)), device_id_type=MESH)
         copy.start()
         first.append(copy)
-    x_ref[0] = effective(0)
-
-    stores = []
-    for mat in range(mats):
-        for copy in full_loads[mat]:
-            copy.wait()
-        nf[mat] = momentum_decay * mf[mat] + gf[mat].astype(jnp.float32)
-        copy = pltpu.make_async_copy(nf.at[mat], newm_hbm.at[mat], store_sem.at[mat])
-        copy.start()
-        stores.append(copy)
+    x_ref[0] = eff_ref[s]
 
     for copy in first:
         copy.wait_recv()
@@ -189,7 +149,6 @@
 
     half = LANES // 2
     low_lanes = lax.broadcasted_iota(jnp.int32, (rows, LANES), 1) < half
-    main = cols - half
     for k in range(shards):
         block = out[k * rows:(k + 1) * rows]
         tiles = [block[:, t * LANES:(t + 1) * LANES] for t in range(chunk // LANES)]
@@ -213,22 +172,40 @@
                 copy.start()
                 third[k, d] = copy
 
+    out_ref[0, 0] = stage[0, c]
     for k in range(shards):
         for d in range(per):
             if k or d:
                 third[k, d].wait_recv()
-                block = recv[k, d].astype(jnp.float32)
-            else:
-                block = stage[0, c].astype(jnp.float32)
-            mat = plane(k) * per + lax.rem(c + per - d, per)
+                out_ref[k, d] = recv[k, d]
+    for copy in first + second + list(third.values()):
+        copy.wait_send()
+
+
+def finish(shards, per, packed_ref, g_ref, m_ref, upd_hbm, newm_hbm, nf, upd, sems):
+    mats, rows, width = g_ref.shape
+    cols = upd.shape[2]
+    half = LANES // 2
+    main = cols - half
+    rep, s = lax.axis_index("rep"), lax.axis_index("shard")
+    c = rep % per
+    copies = []
+    for mat in range(mats):
+        nf[mat] = momentum_decay * m_ref[mat] + g_ref[mat].astype(jnp.float32)
+        copies.append(pltpu.make_async_copy(nf.at[mat], newm_hbm.at[mat], sems.at[mat]))
+        copies[-1].start()
+    for k in range(shards):
+        for d in range(per):
+            block = packed_ref[k, d].astype(jnp.float32)
+            mat = lax.rem(s + k, shards) * per + lax.rem(c + per - d, per)
             lanes = block[rows:, :LANES]
             tail = jnp.concatenate([lanes, pltpu.roll(lanes, half, 1), block[rows:, LANES:2 * LANES]], axis=0)
-            upd_ref[mat, :, :main] = block[:rows].astype(jnp.bfloat16)
-            upd_ref[mat, :, main:] = tail[:, :half].astype(jnp.bfloat16)
-    for copy in stores:
+            upd[mat, :, :main] = block[:rows].astype(jnp.bfloat16)
+            upd[mat, :, main:] = tail[:, :half].astype(jnp.bfloat16)
+    copies.append(pltpu.make_async_copy(upd, upd_hbm, sems.at[mats]))
+    copies[-1].start()
+    for copy in copies:
         copy.wait()
-    for copy in first + second + list(third.values()):
-        copy.wait_send()
 
 
 def per_device_kernel(shards, per, groups, gradients, momentum):
@@ -236,34 +213,51 @@
     chunk = width // groups
     cols = chunk // per
     n = shards * rows
+    scale = 0.2 * math.sqrt(max(n, width))
     packed = (shards, per, rows + 8, cols - LANES // 2)
     f32, bf16, dma = jnp.float32, jnp.bfloat16, pltpu.SemaphoreType.DMA
-    return pl.pallas_call(
-        functools.partial(kernel, shards, per, groups),
-        out_shape=(jax.ShapeDtypeStruct((mats, rows, cols), bf16),
-                   jax.ShapeDtypeStruct((mats, rows, width), f32)),
-        in_specs=[pl.BlockSpec(memory_space=pl.ANY)] * 2,
-        out_specs=(pl.BlockSpec(memory_space=pltpu.VMEM), pl.BlockSpec(memory_space=pl.ANY)),
+    vmem, anywhere = pl.BlockSpec(memory_space=pltpu.VMEM), pl.BlockSpec(memory_space=pl.ANY)
+    rep = lax.axis_index("rep")
+
+    def chunk_of(x):
+        x = x.reshape(shards, per, rows, width)
+        x = lax.dynamic_slice(x, (0, rep % per, 0, rep // per * chunk), (shards, 1, rows, chunk))
+        return x.reshape(shards, rows, chunk)
+
+    grads = chunk_of(gradients).astype(f32)
+    effective = grads + momentum_decay * (momentum_decay * chunk_of(momentum) + grads)
+    blocks = pl.pallas_call(
+        functools.partial(kernel, shards, per, groups, scale),
+        out_shape=jax.ShapeDtypeStruct(packed, bf16),
+        in_specs=[vmem],
+        out_specs=vmem,
         scratch_shapes=[
-            pltpu.VMEM((shards, rows, chunk), bf16),
-            pltpu.VMEM((shards, rows, chunk), f32),
-            pltpu.VMEM((mats, rows, width), bf16),
-            pltpu.VMEM((mats, rows, width), f32),
-            pltpu.VMEM((mats, rows, width), f32),
-            pltpu.VMEM((shards, rows, chunk), f32),
             pltpu.VMEM((shards, rows, chunk), f32),
             pltpu.VMEM((2 * LANES, chunk), bf16),
             pltpu.VMEM((n, LANES), f32),
             pltpu.VMEM((groups, n, LANES), f32),
             pltpu.VMEM(packed, bf16),
             pltpu.VMEM(packed, bf16),
-            dma((2, shards)), dma((2, mats)), dma((mats,)),
             dma((shards,)), dma((shards,)), dma((groups,)), dma((groups,)),
             dma((shards, per)), dma((shards, per)),
         ],
+        cost_estimate=pl.CostEstimate(flops=20_000_000_000, bytes_accessed=1_000_000, transcendentals=0),
         compiler_params=pltpu.CompilerParams(
-            collective_id=0, has_side_effects=True, vmem_limit_bytes=40 * 2**20),
-    )(gradients, momentum)
+            collective_id=0, has_side_effects=True, vmem_limit_bytes=24 * 2**20),
+    )(effective)
+    return pl.pallas_call(
+        functools.partial(finish, shards, per),
+        out_shape=(jax.ShapeDtypeStruct((mats, rows, cols), bf16),
+                   jax.ShapeDtypeStruct((mats, rows, width), f32)),
+        in_specs=[vmem] * 3,
+        out_specs=(anywhere, anywhere),
+        scratch_shapes=[
+            pltpu.VMEM((mats, rows, width), f32),
+            pltpu.VMEM((mats, rows, cols), bf16),
+            dma((mats + 1,)),
+        ],
+        compiler_params=pltpu.CompilerParams(vmem_limit_bytes=24 * 2**20),
+    )(blocks, gradients, momentum)
 
 
 def kernel_fits(shards, replicas, mats, n, width):

time: 31.6 us -> 28 us (0.89)
  local copies, waits for them, and re-layouts: 4.67 us -> 0.01 us
  other arithmetic: 0 us -> 1.08 us
    unnamed x6 -> x4, local copies, waits for them, and re-layouts: 4.67 us -> 0.01 us
    add x0 -> x1, other arithmetic: none -> 1.08 us  [per_device_kernel(): grads + momentum_decay * (momentum_decay * chunk_of(momentum) + grads)]
    pallas_call x1 -> x2, Pallas kernels: 26.1 us -> 26 us  [the longest x1 24.6 us: per_device_kernel(): pl.pallas_call(functools.partial(kernel, shards, per, groups, scale), out...]
where the time goes in v3:
time: 28 us; the launch traced here: 27.8 us
  Pallas kernels  26 us (93%)
  other arithmetic  1.08 us (4%)
  between operations  0.7 us (2%)
    pallas_call x1, Pallas kernels, per_device_kernel(): pl.pallas_call(functools.partial(kernel, shards, per, groups, scale), out...  24.6 us
    pallas_call x1, Pallas kernels, per_device_kernel(): pl.pallas_call(functools.partial(finish, shards, per), out_shape=(jax.Sha...  1.43 us
    add x1, other arithmetic, per_device_kernel(): grads + momentum_decay * (momentum_decay * chunk_of(momentum) + grads)  1.08 us

profile of v3, /device:TPU:0, one launch (start us, length us, event | category | flops | bytes accessed | tf_op | source)
XLA Modules:
  0.0 27.8 jit_solution(10129120415521276875)
XLA Ops:
  0.7 1.1 %convert_add_fusion.eff_ref = f32[4,24,640]{2,1,0:T(8,128)S(1)} fusion(f32[4,2,24,2560]{3,2,1,0:T(8,128)} %bitcast.17, s32[]{:T(128)S(6)} %select_n.23, s32[]{:T(128)S(6)} %select_n.25, bf16[4,2,24,2560]{3,2,1,0:T(8,128)(2,1)} %bitcast.18), kind=kLoop, calls=%fused_computation | loop fusion | flops 307200 | bytes 614408 | tf_op jit(solution)/shard_map/add | solution.py:228
  1.7 0.0 copy-start
  1.8 0.0 copy-start.1
  1.8 24.6 %shard_map.41.packed_ref = bf16[4,2,32,256]{3,2,1,0:T(8,128)(2,1)S(1)} custom-call(f32[4,24,640]{2,1,0:T(8,128)S(1)} %convert_add_fusion.eff_ref), custom_call_target="tpu_custom_call" | custom-call | flops 20000000000 | bytes 1000000 | tf_op jit(solution)/shard_map/pallas_call | solution.py:229
  26.4 0.0 copy-done
  26.4 0.0 copy-done.1
  26.4 1.4 %shard_map.42 = (bf16[8,24,320]{2,1,0:T(8,128)(2,1)}, f32[8,24,2560]{2,1,0:T(8,128)}) custom-call(bf16[4,2,32,256]{3,2,1,0:T(8,128)(2,1)S(1)} %shard_map.41.packed_ref, bf16[8,24,2560]{2,1,0:T(8,128)(2,1)S(1)} %copy-done.1, f32[8,24,2560]{2,1,0:T(8,128)S(1)} %copy-done), custom_call_target="tpu_custom_call" | custom-call | tf_op jit(solution)/shard_map/pallas_call | solution.py:248
Async XLA Ops:
  1.7 24.6 %copy-start = (f32[8,24,2560]{2,1,0:T(8,128)S(1)}, f32[8,24,2560]{2,1,0:T(8,128)}, u32[]{:S(2)}) copy-start(f32[8,24,2560]{2,1,0:T(8,128)} %m_ref.1) | copy-start | bytes 5898244
  1.8 24.6 %copy-start.1 = (bf16[8,24,2560]{2,1,0:T(8,128)(2,1)S(1)}, bf16[8,24,2560]{2,1,0:T(8,128)(2,1)}, u32[]{:S(2)}) copy-start(bf16[8,24,2560]{2,1,0:T(8,128)(2,1)} %g_ref.1) | copy-start | bytes 2949124

commit v4 on v3

--- a/solution.py
+++ b/solution.py
@@ -71,6 +71,17 @@
     return out[:, :n] + out[:, n:]
 
 
+def partner(s, k):
+    for b in range(k.bit_length()):
+        if k >> b & 1:
+            s = s + (1 << b) * (1 - 2 * (s // (1 << b) % 2))
+    return s
+
+
+def far_first(shards):
+    return sorted(range(1, shards), key=lambda k: -k)
+
+
 def kernel(shards, per, groups, scale, eff_ref, out_ref,
            x_ref, xs, part, parts, stage, recv, s1, r1, s2, r2, s3, r3):
     _, rows, chunk = eff_ref.shape
@@ -80,7 +91,7 @@
     j, c = rep // per, rep % per
 
     def plane(k):
-        return lax.rem(s + k, shards)
+        return partner(s, k)
 
     barrier = pltpu.get_barrier_semaphore()
     peers = []
@@ -95,7 +106,7 @@
 
     pl.semaphore_wait(barrier, len(peers))
     first = []
-    for k in range(1, shards):
+    for k in far_first(shards):
         copy = pltpu.make_async_remote_copy(
             src_ref=eff_ref.at[plane(k)], dst_ref=x_ref.at[k], send_sem=s1.at[k], recv_sem=r1.at[k],
             device_id=(rep, plane(k)), device_id_type=MESH)
@@ -161,14 +172,14 @@
             packed = jnp.concatenate([jnp.concatenate(body, axis=1), extra], axis=0)
             stage[k, d] = packed.astype(jnp.bfloat16)
     third = {}
-    for k in [*range(1, shards), 0]:
+    for k in [*far_first(shards), 0]:
         for d in range(per):
             if k or d:
                 core = lax.rem(c + d, per)
                 copy = pltpu.make_async_remote_copy(
                     src_ref=stage.at[k, core], dst_ref=recv.at[k, d],
                     send_sem=s3.at[k, d], recv_sem=r3.at[k, d],
-                    device_id=(j * per + core, plane(shards - k)), device_id_type=MESH)
+                    device_id=(j * per + core, plane(k)), device_id_type=MESH)
                 copy.start()
                 third[k, d] = copy
 
@@ -197,7 +208,7 @@
     for k in range(shards):
         for d in range(per):
             block = packed_ref[k, d].astype(jnp.float32)
-            mat = lax.rem(s + k, shards) * per + lax.rem(c + per - d, per)
+            mat = partner(s, k) * per + lax.rem(c + per - d, per)
             lanes = block[rows:, :LANES]
             tail = jnp.concatenate([lanes, pltpu.roll(lanes, half, 1), block[rows:, LANES:2 * LANES]], axis=0)
             upd[mat, :, :main] = block[:rows].astype(jnp.bfloat16)
@@ -264,6 +275,8 @@
     if mats % shards or n % shards:
         return False
     per, rows = mats // shards, n // shards
+    if shards & (shards - 1):
+        return False
     if per != 2 or rows != 24 or n > LANES or replicas % per:
         return False
     chunk = width * per // replicas

time: 28 us -> 27.3 us (0.975)
  Pallas kernels: 26 us -> 25.3 us
    pallas_call x1, Pallas kernels: 24.6 us -> 23.9 us  [per_device_kernel(): pl.pallas_call(functools.partial(kernel, shards, per, groups, scale), out...]
where the time goes in v4:
time: 27.3 us; the launch traced here: 27.1 us
  Pallas kernels  25.3 us (93%)
  other arithmetic  1.08 us (4%)
  between operations  0.7 us (3%)
    pallas_call x1, Pallas kernels, per_device_kernel(): pl.pallas_call(functools.partial(kernel, shards, per, groups, scale), out...  23.9 us
    pallas_call x1, Pallas kernels, per_device_kernel(): pl.pallas_call(functools.partial(finish, shards, per), out_shape=(jax.Sha...  1.43 us
    add x1, other arithmetic, per_device_kernel(): grads + momentum_decay * (momentum_decay * chunk_of(momentum) + grads)  1.08 us

profile of v4, /device:TPU:0, one launch (start us, length us, event | category | flops | bytes accessed | tf_op | source)
XLA Modules:
  0.0 27.1 jit_solution(12517787734232215671)
XLA Ops:
  0.7 1.1 %convert_add_fusion.eff_ref = f32[4,24,640]{2,1,0:T(8,128)S(1)} fusion(f32[4,2,24,2560]{3,2,1,0:T(8,128)} %bitcast.17, s32[]{:T(128)S(6)} %select_n.23, s32[]{:T(128)S(6)} %select_n.25, bf16[4,2,24,2560]{3,2,1,0:T(8,128)(2,1)} %bitcast.18), kind=kLoop, calls=%fused_computation | loop fusion | flops 307200 | bytes 614408 | tf_op jit(solution)/shard_map/add | solution.py:239
  1.7 0.0 copy-start
  1.8 0.0 copy-start.1
  1.8 23.9 %shard_map.41.packed_ref = bf16[4,2,32,256]{3,2,1,0:T(8,128)(2,1)S(1)} custom-call(f32[4,24,640]{2,1,0:T(8,128)S(1)} %convert_add_fusion.eff_ref), custom_call_target="tpu_custom_call" | custom-call | flops 20000000000 | bytes 1000000 | tf_op jit(solution)/shard_map/pallas_call | solution.py:240
  25.7 0.0 copy-done
  25.7 0.0 copy-done.1
  25.7 1.4 %shard_map.42 = (bf16[8,24,320]{2,1,0:T(8,128)(2,1)}, f32[8,24,2560]{2,1,0:T(8,128)}) custom-call(bf16[4,2,32,256]{3,2,1,0:T(8,128)(2,1)S(1)} %shard_map.41.packed_ref, bf16[8,24,2560]{2,1,0:T(8,128)(2,1)S(1)} %copy-done.1, f32[8,24,2560]{2,1,0:T(8,128)S(1)} %copy-done), custom_call_target="tpu_custom_call" | custom-call | tf_op jit(solution)/shard_map/pallas_call | solution.py:259
Async XLA Ops:
  1.7 23.9 %copy-start = (f32[8,24,2560]{2,1,0:T(8,128)S(1)}, f32[8,24,2560]{2,1,0:T(8,128)}, u32[]{:S(2)}) copy-start(f32[8,24,2560]{2,1,0:T(8,128)} %m_ref.1) | copy-start | bytes 5898244
  1.8 23.9 %copy-start.1 = (bf16[8,24,2560]{2,1,0:T(8,128)(2,1)S(1)}, bf16[8,24,2560]{2,1,0:T(8,128)(2,1)}, u32[]{:S(2)}) copy-start(bf16[8,24,2560]{2,1,0:T(8,128)(2,1)} %g_ref.1) | copy-start | bytes 2949124
